TPU v7x, 32 devices: a whole 2x2x4 slice. The times are simulated.
32 devices in a mesh: ctx: 16 (over z, y, x), head: 2 (over core).
Axes of the slice: x: 2, y: 2, z: 4, core: 2. Of those that a mesh axis runs over, the one named last changes fastest.
Arguments:
- fresh_query: bfloat16 [256, 768], P('ctx', 'head'), may hold values from -64 to 64
- fresh_key: bfloat16 [256, 768], P('ctx', 'head'), may hold values from -2.5 to 2.5
- fresh_value: bfloat16 [256, 768], P('ctx', 'head'), may hold values from -6 to 6
- cache_key: bfloat16 [4096, 768], P('ctx', 'head'), may hold values from -6 to 6
- cache_value: bfloat16 [4096, 768], P('ctx', 'head'), may hold values from -6 to 6
- slot_owner: int32 [16], replicated, may hold values from 0 to 15, each once
- evictor: int32 [1], replicated, may hold values from 0 to 15
- timestep: int32 [1], replicated, may hold values from 0 to 49
- age_slope: float32 [6], P('head'), may hold values from 0.5 to 4
- time_gate: float32 [50, 768], P(None, 'head'), may hold values from 0.5 to 2
Outputs:
- attn_output: bfloat16 [256, 768], P('ctx', 'head')
- next_key: bfloat16 [4096, 768], P('ctx', 'head')
- next_value: bfloat16 [4096, 768], P('ctx', 'head')
Inputs may be any that keep to these rules, and one draw needn't show every extreme that they name: `slot_owner`: a permutation of the 16 owners.
All inputs are finite; a program needn't handle non-finite values.
Results may differ from a plain program's by a relative error of at most 0.003.
Values may be sent and summed in bfloat16 or wider, within the bound.
A program may use at most 64 MiB of HBM per device.

v0:
```python
import math

import jax
import jax.numpy as jnp
from jax import lax
from jax.sharding import PartitionSpec as P


def body(
    fresh_query,
    fresh_key,
    fresh_value,
    cache_key,
    cache_value,
    slot_owner,
    evictor,
    timestep,
    age_slope,
    time_gate,
):
    feature_width = fresh_query.shape[1]
    heads_here = age_slope.shape[0]
    head_dim = feature_width // heads_here
    owners = lax.axis_size("ctx")
    owner_index = lax.axis_index("ctx")
    queries = lax.all_gather(fresh_query, "ctx", axis=0, tiled=True)
    total_rows = queries.shape[0]
    block_rows = min(512, total_rows)
    blocks = total_rows // block_rows
    slot_ids = jnp.arange(owners, dtype=jnp.int32)
    slot_rank = jnp.sum(jnp.where(slot_owner == owner_index, slot_ids, 0))
    cache_age = (slot_rank + 1).astype(jnp.float32) / owners
    local_keys = jnp.concatenate([fresh_key, cache_key], 0)
    local_values = jnp.concatenate([fresh_value, cache_value], 0)
    key_count = local_keys.shape[0]
    key_age = jnp.where(jnp.arange(key_count) >= fresh_key.shape[0], cache_age, 0.0)
    penalty = (age_slope[:, None] * key_age[None, :])[:, None, :]
    head_keys = local_keys.reshape(key_count, heads_here, head_dim)
    head_values = local_values.reshape(key_count, heads_here, head_dim)
    query_blocks = queries.reshape(blocks, block_rows, heads_here, head_dim)
    score_scale = 1.0 / math.sqrt(head_dim)

    def weigh_block(query_block):
        scores = (
            jnp.einsum("qhd,khd->hqk", query_block, head_keys, preferred_element_type=jnp.float32)
            * score_scale
            - penalty
        )
        largest = jnp.max(scores, axis=2)
        weights = jnp.exp(scores - largest[:, :, None]).astype(jnp.bfloat16)
        denominator = jnp.sum(weights.astype(jnp.float32), axis=2)
        numerator = jnp.einsum(
            "hqk,khd->qhd", weights, head_values, preferred_element_type=jnp.float32
        )
        return (numerator.reshape(block_rows, feature_width), denominator.T, largest.T)

    numerators, denominators, maxima = lax.map(weigh_block, query_blocks)
    numerators = numerators.reshape(total_rows, feature_width)
    denominators = denominators.reshape(total_rows, heads_here)
    maxima = maxima.reshape(total_rows, heads_here)
    row_max = lax.pmax(maxima, "ctx")
    factor = jnp.exp(maxima - row_max)
    scaled_numer = (
        numerators.reshape(total_rows, heads_here, head_dim) * factor[:, :, None]
    ).reshape(total_rows, feature_width)
    scaled_denom = denominators * factor
    own_numer, own_denom = (
        lax.psum_scatter(scaled_numer, "ctx", scatter_dimension=0, tiled=True),
        lax.psum_scatter(scaled_denom, "ctx", scatter_dimension=0, tiled=True),
    )
    rows_here = own_numer.shape[0]
    own_numer = own_numer.reshape(rows_here, heads_here, head_dim)
    attended = (own_numer / own_denom[:, :, None]).reshape(rows_here, feature_width)
    squares = lax.psum(jnp.sum(attended * attended, axis=1), "head")
    inverse = lax.rsqrt(squares / (feature_width * lax.axis_size("head")) + 1e-06)
    picked = jnp.arange(time_gate.shape[0]) == timestep[0]
    gate_row = jnp.sum(jnp.where(picked[:, None], time_gate, 0.0), axis=0)
    attn_output = (attended * inverse[:, None] * gate_row[None, :]).astype(jnp.bfloat16)
    fresh_keys, fresh_values = (
        lax.all_gather(fresh_key, "ctx", axis=0, tiled=True),
        lax.all_gather(fresh_value, "ctx", axis=0, tiled=True),
    )
    evicted = owner_index == evictor[0]
    next_key = jnp.where(evicted, fresh_keys, cache_key)
    next_value = jnp.where(evicted, fresh_values, cache_value)
    return (attn_output, next_key, next_value)


def solution(mesh):
    return jax.shard_map(
        body,
        mesh=mesh,
        in_specs=(
            P("ctx", "head"),
            P("ctx", "head"),
            P("ctx", "head"),
            P("ctx", "head"),
            P("ctx", "head"),
            P(),
            P(),
            P(),
            P("head"),
            P(None, "head"),
        ),
        out_specs=(P("ctx", "head"), P("ctx", "head"), P("ctx", "head")),
        check_vma=False,
    )
```

profile of v0, /device:TPU:0, one launch (start us, length us, event | category | flops | bytes accessed | tf_op | source)
XLA Modules:
  0.0 299.8 jit_solution(15910894297494697371)
XLA Ops:
  7.2 0.0 copy-start.6
  7.2 0.0 reduce-scatter.7.cloned.1.call-start
  7.2 1.3 fusion.8
  9.2 0.0 copy-done.6
  9.2 43.4 %all_gather.9 = bf16[256,384]{1,0:T(8,128)(2,1)S(1)} all-gather(bf16[16,384]{1,0:T(8,128)(2,1)S(1)} %copy-done.6), channel_id=1, replica_groups=mesh['ctx'=16,'head'=2] {'ctx'}, dimensions={0}, use_global_device_ids=true | all-gather | bytes 208896 | tf_op jit(solution)/shard_map/all_gather | solution.py:26
  52.6 0.0 copy-start.7
  52.6 0.0 copy-start
  52.6 0.0 copy-start.5
  52.6 0.1 copy.21
  52.8 0.5 copy-done.7
  53.3 0.1 broadcast_multiply_fusion
  53.3 0.2 copy-done
  53.6 0.0 copy-done.5
  53.6 0.3 fusion.9
  53.8 0.1 convert_reduce_fusion
  54.0 0.0 copy-start.1
  54.0 36.7 %pmax.7 = f32[256,3]{0,1:T(4,128)S(1)} all-reduce(f32[256,3]{0,1:T(4,128)S(1)} %bitcast.46), channel_id=1, replica_groups=mesh['ctx'=16,'head'=2] {'ctx'}, use_global_device_ids=true, to_apply=%region_2.3 | all-reduce | flops 768 | bytes 6144 | tf_op jit(solution)/shard_map/pmax | solution.py:61
  90.7 0.8 copy.28
  91.5 0.0 copy-start.4
  91.5 0.0 reduce-scatter.7.cloned.1.call-update
  91.6 0.0 reduce-scatter.5.cloned.1.call-start
  91.6 0.0 copy-done.1
  91.6 0.6 copy-done.4
  92.2 0.3 fusion.2
  92.6 0.9 copy.25
  93.5 0.0 reduce-scatter.5.cloned.1.call-update
  93.5 38.5 %all_gather.11 = bf16[256,384]{1,0:T(8,128)(2,1)S(1)} all-gather(bf16[16,384]{1,0:T(8,128)(2,1)S(1)} %copy-done.4), channel_id=1, replica_groups=mesh['ctx'=16,'head'=2] {'ctx'}, dimensions={0}, use_global_device_ids=true | all-gather | bytes 208896 | tf_op jit(solution)/shard_map/all_gather | solution.py:81
  133.4 0.0 copy-start.3
  133.4 36.7 %all_gather.10 = bf16[256,384]{1,0:T(8,128)(2,1)S(1)} all-gather(bf16[16,384]{1,0:T(8,128)(2,1)S(1)} %copy-done.5), channel_id=1, replica_groups=mesh['ctx'=16,'head'=2] {'ctx'}, dimensions={0}, use_global_device_ids=true | all-gather | bytes 208896 | tf_op jit(solution)/shard_map/all_gather | solution.py:80
  170.1 0.0 copy-done.3
  170.1 0.1 select_reduce_fusion
  170.2 0.7 broadcast_select_fusion
  170.9 0.7 broadcast_select_fusion.1
  171.6 0.0 reduce-scatter.7.cloned.1.call-done
  171.6 117.3 %reduce-scatter.5.cloned.1.call-done = f32[16,384]{1,0:T(8,128)} async-done(((f32[256,384]{1,0:T(8,128)}), f32[16,384]{1,0:T(8,128)}) %reduce-scatter.5.cloned.1.call-update) | async-done | bytes 24592 | tf_op jit(solution)/shard_map/reduce_scatter | solution.py:68
  288.9 0.0 copy-start.2
  288.9 0.8 div.18
  289.7 0.0 copy-done.2
  289.7 0.1 multiply_reduce_fusion
  289.8 2.5 psum.7
  292.3 0.7 multiply_convert_fusion
  (4 shorter events, 0.0 us)
Async XLA Ops:
  7.2 2.0 copy-start.6
  7.2 164.4 %reduce-scatter.7.cloned.1.call-start = ((), (), s32[]{:S(2)}) async-start(), calls=%async_computation.3 | async-start | bytes 139264 | tf_op jit(solution)/shard_map/reduce_scatter | solution.py:69
  52.6 0.7 copy-start.7
  52.6 0.9 copy-start
  52.6 0.9 copy-start.5
  54.0 37.6 %copy-start.1 = (bf16[256,384]{1,0:T(8,128)(2,1)S(1)}, bf16[256,384]{1,0:T(8,128)(2,1)}, u32[]{:S(2)}) copy-start(bf16[256,384]{1,0:T(8,128)(2,1)} %param.14) | copy-start | bytes 589828
  91.5 0.7 copy-start.4
  91.6 197.4 %reduce-scatter.5.cloned.1.call-start = ((), (), s32[]{:S(2)}) async-start(), calls=%async_computation.2 | async-start | bytes 417792 | tf_op jit(solution)/shard_map/reduce_scatter | solution.py:68
  133.4 36.7 %copy-start.3 = (f32[50,384]{1,0:T(8,128)S(1)}, f32[50,384]{1,0:T(8,128)}, u32[]{:S(2)}) copy-start(f32[50,384]{1,0:T(8,128)} %param.19) | copy-start | bytes 230404
  288.9 0.8 copy-start.2
Sparse Core Ops, SparseCore 0:
  91.7 73.8 reduce-scatter.6
  171.0 117.9 reduce-scatter.4
where the time goes:
time: 300 us
  blocking collectives  158 us (53%)
  waiting for transfers between devices  117 us (39%)
  between operations  16.1 us (5%)
  local copies, waits for them, and re-layouts  4 us (1%)
  other arithmetic  3.83 us (1%)
    reduce_scatter x1, waiting for transfers between devices, body(): lax.psum_scatter(scaled_numer, 'ctx', scatter_dimension=0, tiled=True)  117 us
    all_gather x1, blocking collectives, body(): queries = lax.all_gather(fresh_query, 'ctx', axis=0, tiled=True)  43.4 us
    all_gather x1, blocking collectives, body(): lax.all_gather(fresh_value, 'ctx', axis=0, tiled=True)  38.5 us
    pmax x1, blocking collectives, body(): row_max = lax.pmax(maxima, 'ctx')  36.7 us
    all_gather x1, blocking collectives, body(): lax.all_gather(fresh_key, 'ctx', axis=0, tiled=True)  36.7 us
  transfers between devices with their start and end apart: 2, of which 1 were waited for; matrix products, arithmetic and copies ran while one was open for 1% of the time, Pallas kernels for 0%

commit v1 on v0

v1 whole, which is shorter than its diff:
```python
import functools
import math

import jax
import jax.numpy as jnp
from jax import lax
from jax.experimental import pallas as pl
from jax.experimental.pallas import tpu as pltpu
from jax.sharding import PartitionSpec as P

MESH = pl.DeviceIdType.MESH
PLANES = 4
LANES = 128


def kernel(
    owners,
    head_devices,
    slot_ref,
    step_ref,
    slope_ref,
    query_in,
    key_in,
    value_in,
    cache_key_in,
    cache_value_in,
    gate_in,
    out_ref,
    all_keys,
    all_values,
    gath_key,
    gath_value,
    queries,
    keys,
    values,
    gate,
    sent,
    received,
    squares,
    local_sem,
    query_send,
    query_recv,
    part_send,
    part_recv,
    col_send,
    col_recv,
    plane_send,
    plane_recv,
    square_send,
    square_recv,
):
    rows, width = query_in.shape
    cache_rows = cache_key_in.shape[0]
    heads = slope_ref.shape[0]
    head_dim = width // heads
    plane = owners // PLANES
    me = lax.axis_index("ctx")
    my_head = lax.axis_index("head")
    my_z = me // plane
    my_p = lax.rem(me, plane)
    key_rows = keys.shape[0]

    barrier = pltpu.get_barrier_semaphore()

    def greet(step, carry):
        peer = lax.rem(me + step, owners)
        pl.semaphore_signal(barrier, inc=1, device_id=(peer, my_head), device_id_type=MESH)
        return carry

    lax.fori_loop(1, owners, greet, 0)
    for step in range(1, head_devices):
        peer = lax.rem(my_head + step, head_devices)
        pl.semaphore_signal(barrier, inc=1, device_id=(me, peer), device_id_type=MESH)

    locals_ = [
        pltpu.make_async_copy(query_in, queries.at[0], local_sem.at[0]),
        pltpu.make_async_copy(cache_key_in, keys.at[pl.ds(0, cache_rows)], local_sem.at[1]),
        pltpu.make_async_copy(key_in, keys.at[pl.ds(cache_rows, rows)], local_sem.at[2]),
        pltpu.make_async_copy(cache_value_in, values.at[pl.ds(0, cache_rows)], local_sem.at[3]),
        pltpu.make_async_copy(value_in, values.at[pl.ds(cache_rows, rows)], local_sem.at[4]),
        pltpu.make_async_copy(gate_in, gate, local_sem.at[5]),
        pltpu.make_async_copy(key_in, gath_key.at[0, 0], local_sem.at[6]),
        pltpu.make_async_copy(value_in, gath_value.at[0, 0], local_sem.at[7]),
    ]
    for copy in locals_:
        copy.start()
    spare = key_rows - cache_rows - rows
    keys[pl.ds(cache_rows + rows, spare), :] = jnp.zeros((spare, width), jnp.bfloat16)
    values[pl.ds(cache_rows + rows, spare), :] = jnp.zeros((spare, width), jnp.bfloat16)

    pl.semaphore_wait(barrier, owners - 1 + head_devices - 1)

    def device(dz, dp):
        z = lax.rem(my_z + dz + PLANES, PLANES)
        return (z * plane + lax.rem(my_p + dp + plane, plane), my_head)

    def query_copy(dz, dp):
        slot = dz * plane + dp
        return pltpu.make_async_remote_copy(
            src_ref=query_in,
            dst_ref=queries.at[slot],
            send_sem=query_send.at[slot],
            recv_sem=query_recv.at[slot],
            device_id=device(dz, dp),
            device_id_type=MESH,
        )

    def part_copy(dz, dp):
        slot = dz * plane + dp
        return pltpu.make_async_remote_copy(
            src_ref=sent.at[slot],
            dst_ref=received.at[slot],
            send_sem=part_send.at[slot],
            recv_sem=part_recv.at[slot],
            device_id=device(-dz, -dp),
            device_id_type=MESH,
        )

    def col_copy(kind, dz):
        return pltpu.make_async_remote_copy(
            src_ref=(key_in, value_in)[kind],
            dst_ref=(gath_key, gath_value)[kind].at[0, dz],
            send_sem=col_send.at[kind * PLANES + dz],
            recv_sem=col_recv.at[kind * PLANES + dz],
            device_id=device(dz, 0),
            device_id_type=MESH,
        )

    def plane_copy(kind, dp):
        gathered = (gath_key, gath_value)[kind]
        return pltpu.make_async_remote_copy(
            src_ref=gathered.at[0],
            dst_ref=gathered.at[dp],
            send_sem=plane_send.at[kind * plane + dp],
            recv_sem=plane_recv.at[kind * plane + dp],
            device_id=device(0, dp),
            device_id_type=MESH,
        )

    def peers(dz):
        return range(0 if dz else 1, plane)

    for dz in range(PLANES):
        for dp in peers(dz):
            query_copy(dz, dp).start()
    for dz in range(1, PLANES):
        for kind in range(2):
            col_copy(kind, dz).start()

    slot_rank = jnp.int32(0)
    for slot in range(owners):
        slot_rank += jnp.where(slot_ref[slot] == me, slot, 0)
    age = (slot_rank + 1).astype(jnp.float32) * (1.0 / owners)
    scale = 1.0 / math.sqrt(head_dim)
    tokens = plane * rows
    column = lax.broadcasted_iota(jnp.int32, (1, key_rows), 1)
    lane = lax.broadcasted_iota(jnp.int32, (tokens, LANES), 1)
    group, piece = lane >> 3, lane & 7
    ones = jnp.ones((key_rows, LANES), jnp.bfloat16)

    def weigh(dz):
        slots = slice(dz * plane, (dz + 1) * plane)
        query = queries[slots].reshape(tokens, width)
        stat = jnp.zeros((tokens, LANES), jnp.float32)
        for head in range(heads):
            cut = slice(head * head_dim, (head + 1) * head_dim)
            penalty = jnp.where(
                column < cache_rows,
                slope_ref[head] * age,
                jnp.where(column < cache_rows + rows, 0.0, 1e30),
            )
            scores = (
                lax.dot_general(
                    query[:, cut],
                    keys[:, cut],
                    (((1,), (1,)), ((), ())),
                    preferred_element_type=jnp.float32,
                )
                * scale
                - penalty
            )
            largest = jnp.max(scores, axis=1, keepdims=True)
            weights = jnp.exp(scores - largest).astype(jnp.bfloat16)
            both = jnp.dot(
                weights,
                jnp.concatenate([values[:, cut], ones], axis=1),
                preferred_element_type=jnp.float32,
            )
            numer, denom = both[:, :head_dim], both[:, head_dim:]
            sent[slots, :, cut] = numer.astype(jnp.bfloat16).reshape(plane, rows, head_dim)
            stat = jnp.where(group == head, jnp.where(piece < 3, largest, denom), stat)
        high = stat.astype(jnp.bfloat16).astype(jnp.float32)
        rest = stat - high
        middle = rest.astype(jnp.bfloat16).astype(jnp.float32)
        low = rest - middle
        third = jnp.where(piece < 3, piece, piece - 3)
        cuts = jnp.where(third == 0, high, jnp.where(third == 1, middle, low))
        sent[slots, :, width:] = cuts.astype(jnp.bfloat16).reshape(plane, rows, LANES)

    for copy in locals_:
        copy.wait()

    for dz in range(PLANES):
        for dp in peers(dz):
            query_copy(dz, dp).wait_recv()
        weigh(dz)
        for dp in peers(dz):
            part_copy(dz, dp).start()
    received[0] = sent[0]

    for kind in range(2):
        for dz in range(1, PLANES):
            col_copy(kind, dz).wait_recv()
        for dp in peers(0):
            plane_copy(kind, dp).start()

    for dz in range(PLANES):
        for dp in peers(dz):
            part_copy(dz, dp).wait_recv()

    stats = received[:, :, width:].astype(jnp.float32).reshape(owners * rows, LANES)
    stats = (
        stats
        + pltpu.roll(stats, LANES - 1, axis=1)
        + pltpu.roll(stats, LANES - 2, axis=1)
    )
    denoms = pltpu.roll(stats, LANES - 3, axis=1).reshape(owners, rows, LANES)
    maxima = stats.reshape(owners, rows, LANES)
    factor = jnp.exp(maxima - jnp.max(maxima, axis=0, keepdims=True))
    share = factor / jnp.sum(factor * denoms, axis=0, keepdims=True)
    attended = []
    for head in range(heads):
        cut = slice(head * head_dim, (head + 1) * head_dim)
        attended.append(
            jnp.sum(
                share[:, :, 8 * head : 8 * head + 1] * received[:, :, cut].astype(jnp.float32),
                axis=0,
            )
        )
    total = attended[0] * attended[0]
    for block in attended[1:]:
        total += block * block
    squares[0] = jnp.broadcast_to(jnp.sum(total, axis=1, keepdims=True), (rows, LANES))

    def square_copy(step):
        return pltpu.make_async_remote_copy(
            src_ref=squares.at[0],
            dst_ref=squares.at[step],
            send_sem=square_send.at[step],
            recv_sem=square_recv.at[step],
            device_id=(me, lax.rem(my_head + step, head_devices)),
            device_id_type=MESH,
        )

    for step in range(1, head_devices):
        square_copy(step).start()
    for dz in range(PLANES):
        for dp in peers(dz):
            query_copy(dz, dp).wait_send()
            part_copy(dz, dp).wait_send()
    moment = lax.broadcasted_iota(jnp.int32, gate.shape, 0) == step_ref[0]
    gate_row = jnp.sum(jnp.where(moment, gate[...], 0.0), axis=0, keepdims=True)
    for kind in range(2):
        for dz in range(1, PLANES):
            col_copy(kind, dz).wait_send()
        for dp in peers(0):
            plane_copy(kind, dp).wait_recv()
    for dz in range(PLANES):
        z = lax.rem(my_z - dz + PLANES, PLANES)
        for dp in range(plane):
            p = lax.rem(my_p - dp + plane, plane)
            all_keys[z, p] = gath_key[dp, dz]
            all_values[z, p] = gath_value[dp, dz]
    for step in range(1, head_devices):
        square_copy(step).wait_recv()
    mean = jnp.sum(squares[...], axis=0) * (1.0 / (width * head_devices))
    inverse = lax.rsqrt(mean + 1e-06)
    for head in range(heads):
        cut = slice(head * head_dim, (head + 1) * head_dim)
        out_ref[:, cut] = (attended[head] * inverse * gate_row[:, cut]).astype(jnp.bfloat16)

    for step in range(1, head_devices):
        square_copy(step).wait_send()
    for kind in range(2):
        for dp in peers(0):
            plane_copy(kind, dp).wait_send()


def body(
    fresh_query,
    fresh_key,
    fresh_value,
    cache_key,
    cache_value,
    slot_owner,
    evictor,
    timestep,
    age_slope,
    time_gate,
):
    rows, width = fresh_query.shape
    cache_rows = cache_key.shape[0]
    owners = lax.axis_size("ctx")
    head_devices = lax.axis_size("head")
    plane = owners // PLANES
    key_rows = cache_rows + LANES * pl.cdiv(rows, LANES)
    smem = pl.BlockSpec(memory_space=pltpu.SMEM)
    vmem = pl.BlockSpec(memory_space=pltpu.VMEM)
    anywhere = pl.BlockSpec(memory_space=pltpu.HBM)
    bf16 = jnp.bfloat16
    dma = pltpu.SemaphoreType.DMA
    gathered = jax.ShapeDtypeStruct((PLANES, plane, rows, width), bf16)
    attn_output, fresh_keys, fresh_values = pl.pallas_call(
        functools.partial(kernel, owners, head_devices),
        out_shape=(jax.ShapeDtypeStruct((rows, width), bf16), gathered, gathered),
        in_specs=[smem] * 3 + [anywhere] * 6,
        out_specs=(vmem, vmem, vmem),
        scratch_shapes=[
            pltpu.VMEM((plane, PLANES, rows, width), bf16),
            pltpu.VMEM((plane, PLANES, rows, width), bf16),
            pltpu.VMEM((owners, rows, width), bf16),
            pltpu.VMEM((key_rows, width), bf16),
            pltpu.VMEM((key_rows, width), bf16),
            pltpu.VMEM(time_gate.shape, jnp.float32),
            pltpu.VMEM((owners, rows, width + LANES), bf16),
            pltpu.VMEM((owners, rows, width + LANES), bf16),
            pltpu.VMEM((head_devices, rows, LANES), jnp.float32),
            dma((8,)),
            dma((owners,)),
            dma((owners,)),
            dma((owners,)),
            dma((owners,)),
            dma((2 * PLANES,)),
            dma((2 * PLANES,)),
            dma((2 * plane,)),
            dma((2 * plane,)),
            dma((head_devices,)),
            dma((head_devices,)),
        ],
        compiler_params=pltpu.CompilerParams(
            collective_id=0, has_side_effects=True, vmem_limit_bytes=60 * 1024 * 1024
        ),
        name="attend",
    )(
        slot_owner,
        timestep,
        age_slope,
        fresh_query,
        fresh_key,
        fresh_value,
        cache_key,
        cache_value,
        time_gate,
    )
    evicted = lax.axis_index("ctx") == evictor[0]

    def rolled(gathered, cache):
        return jnp.where(evicted, gathered.reshape(cache.shape), cache)

    next_key, next_value = rolled(fresh_keys, cache_key), rolled(fresh_values, cache_value)
    return (attn_output, next_key, next_value)


def solution(mesh):
    return jax.shard_map(
        body,
        mesh=mesh,
        in_specs=(
            P("ctx", "head"),
            P("ctx", "head"),
            P("ctx", "head"),
            P("ctx", "head"),
            P("ctx", "head"),
            P(),
            P(),
            P(),
            P("head"),
            P(None, "head"),
        ),
        out_specs=(P("ctx", "head"), P("ctx", "head"), P("ctx", "head")),
        check_vma=False,
    )
```

time: 300 us -> 33.8 us (0.11)
  blocking collectives: 158 us -> 0 us
  waiting for transfers between devices: 117 us -> 0 us
  Pallas kernels: 0 us -> 29.2 us
  between operations: 16.1 us -> 1.98 us
  local copies, waits for them, and re-layouts: 4 us -> 0.61 us
    all_gather x3 -> x0, blocking collectives: 119 us -> none  [the longest x1 43.4 us: body(): queries = lax.all_gather(fresh_query, 'ctx', axis=0, tiled=True)]
    reduce_scatter x2 -> x0, waiting for transfers between devices: 117 us -> none  [the longest x1 117 us: body(): lax.psum_scatter(scaled_numer, 'ctx', scatter_dimension=0, tiled=True)]
    pmax x1 -> x0, blocking collectives: 36.7 us -> none  [body(): row_max = lax.pmax(maxima, 'ctx')]
    pallas_call x0 -> x1, Pallas kernels: none -> 29.2 us  [body(): pl.pallas_call(functools.partial(kernel, owners, head_devices), out_shape...]
  transfers between devices with their start and end apart: 2 -> 0, of which waited for: 1 -> 0; matrix products, arithmetic and copies ran while one was open for 1% -> 0% of each run, Pallas kernels for 0% -> 0%
where the time goes in v1:
time: 33.8 us; the launch traced here: 33.6 us
  Pallas kernels  29.2 us (86%)
  between operations  1.98 us (6%)
  other arithmetic  1.82 us (5%)
  local copies, waits for them, and re-layouts  0.61 us (2%)
    pallas_call x1, Pallas kernels, body(): pl.pallas_call(functools.partial(kernel, owners, head_devices), out_shape...  29.2 us
    select_n x1, other arithmetic, rolled(): return jnp.where(evicted, gathered.reshape(cache.shape), cache)  1.82 us

profile of v1, /device:TPU:0, one launch (start us, length us, event | category | flops | bytes accessed | tf_op | source)
XLA Modules:
  0.0 33.6 jit_solution(11714777483645208461)
XLA Ops:
  1.9 0.0 copy-start
  1.9 0.0 copy-start.1
  1.9 29.2 %attend.1 = (bf16[16,384]{1,0:T(8,128)(2,1)}, bf16[4,4,16,384]{3,2,1,0:T(8,128)(2,1)}, bf16[4,4,16,384]{3,2,1,0:T(8,128)(2,1)}) custom-call(s32[16]{0:T(128)} %slot_ref.1, s32[1]{0:T(128)S(6)} %copy.15.step_ref, f32[3]{0:T(128)} %slope_ref.1, bf16[16,384]{1,0:T(8,128)(2,1)} %query_in.1, bf16[16,384]{1,0:T(8,128)(2,1)} %key_in.1, bf16[16,384]{1,0:T(8,128)(2,1)} %value_in.1, ...), custom_call_target="tpu_custom_call" | custom-call | tf_op jit(solution)/shard_map/attend/pallas_call | solution.py:313
  31.1 0.0 copy-done
  31.2 0.0 copy-done.1
  31.2 0.0 copy-start.2
  31.2 1.8 %bitcast_select_fusion = (bf16[256,384]{1,0:T(8,128)(2,1)}, bf16[256,384]{1,0:T(8,128)(2,1)}) fusion(bf16[256,384]{1,0:T(8,128)(2,1)S(1)} %copy-done.1, bf16[4,4,16,384]{3,2,1,0:T(8,128)(2,1)} %get-tuple-element.8, pred[]{:T(512)S(6)} %eq.3, bf16[256,384]{1,0:T(8,128)(2,1)S(1)} %copy-done, bf16[4,4,16,384]{3,2,1,0:T(8,128)(2,1)} %get-tuple-element.7), kind=kLoop, calls=%fused_computation | loop fusion | flops 196608 | bytes 1179649 | tf_op jit(solution)/shard_map/jit(_where)/select_n | solution.py:358
  33.0 0.0 copy-done.2
  33.0 0.6 %copy.16 = bf16[16,384]{1,0:T(8,128)(2,1)} copy(bf16[16,384]{1,0:T(8,128)(2,1)S(1)} %copy-done.2) | data formatting | bytes 24576
Async XLA Ops:
  1.9 29.2 %copy-start = (bf16[256,384]{1,0:T(8,128)(2,1)S(1)}, bf16[256,384]{1,0:T(8,128)(2,1)}, u32[]{:S(2)}) copy-start(bf16[256,384]{1,0:T(8,128)(2,1)} %cache_key_in.1) | copy-start | bytes 589828
  1.9 29.2 %copy-start.1 = (bf16[256,384]{1,0:T(8,128)(2,1)S(1)}, bf16[256,384]{1,0:T(8,128)(2,1)}, u32[]{:S(2)}) copy-start(bf16[256,384]{1,0:T(8,128)(2,1)} %cache_value_in.1) | copy-start | bytes 589828
  31.2 1.8 %copy-start.2 = (bf16[16,384]{1,0:T(8,128)(2,1)S(1)}, bf16[16,384]{1,0:T(8,128)(2,1)}, u32[]{:S(2)}) copy-start(bf16[16,384]{1,0:T(8,128)(2,1)} %get-tuple-element.14) | copy-start | bytes 36868

commit v2 on v1

--- a/solution.py
+++ b/solution.py
@@ -26,6 +26,8 @@
     cache_value_in,
     gate_in,
     out_ref,
+    keys_out,
+    values_out,
     all_keys,
     all_values,
     gath_key,
@@ -94,19 +96,19 @@
         z = lax.rem(my_z + dz + PLANES, PLANES)
         return (z * plane + lax.rem(my_p + dp + plane, plane), my_head)
 
-    def query_copy(dz, dp):
-        slot = dz * plane + dp
+    def query_copy(dz, dp, relayed=False):
+        slot = dp * PLANES + dz
         return pltpu.make_async_remote_copy(
-            src_ref=query_in,
+            src_ref=queries.at[dz] if relayed else query_in,
             dst_ref=queries.at[slot],
             send_sem=query_send.at[slot],
             recv_sem=query_recv.at[slot],
-            device_id=device(dz, dp),
+            device_id=device(0 if relayed else dz, dp),
             device_id_type=MESH,
         )
 
     def part_copy(dz, dp):
-        slot = dz * plane + dp
+        slot = dp * PLANES + dz
         return pltpu.make_async_remote_copy(
             src_ref=sent.at[slot],
             dst_ref=received.at[slot],
@@ -137,12 +139,12 @@
             device_id_type=MESH,
         )
 
-    def peers(dz):
-        return range(0 if dz else 1, plane)
-
-    for dz in range(PLANES):
-        for dp in peers(dz):
-            query_copy(dz, dp).start()
+    others = [(dz, dp) for dp in range(plane) for dz in range(PLANES) if dz or dp]
+
+    for dz in range(1, PLANES):
+        query_copy(dz, 0).start()
+    for dp in range(1, plane):
+        query_copy(0, dp).start()
     for dz in range(1, PLANES):
         for kind in range(2):
             col_copy(kind, dz).start()
@@ -152,14 +154,14 @@
         slot_rank += jnp.where(slot_ref[slot] == me, slot, 0)
     age = (slot_rank + 1).astype(jnp.float32) * (1.0 / owners)
     scale = 1.0 / math.sqrt(head_dim)
-    tokens = plane * rows
+    tokens = PLANES * rows
     column = lax.broadcasted_iota(jnp.int32, (1, key_rows), 1)
     lane = lax.broadcasted_iota(jnp.int32, (tokens, LANES), 1)
     group, piece = lane >> 3, lane & 7
     ones = jnp.ones((key_rows, LANES), jnp.bfloat16)
 
-    def weigh(dz):
-        slots = slice(dz * plane, (dz + 1) * plane)
+    def weigh(dp):
+        slots = slice(dp * PLANES, (dp + 1) * PLANES)
         query = queries[slots].reshape(tokens, width)
         stat = jnp.zeros((tokens, LANES), jnp.float32)
         for head in range(heads):
@@ -187,7 +189,7 @@
                 preferred_element_type=jnp.float32,
             )
             numer, denom = both[:, :head_dim], both[:, head_dim:]
-            sent[slots, :, cut] = numer.astype(jnp.bfloat16).reshape(plane, rows, head_dim)
+            sent[slots, :, cut] = numer.astype(jnp.bfloat16).reshape(PLANES, rows, head_dim)
             stat = jnp.where(group == head, jnp.where(piece < 3, largest, denom), stat)
         high = stat.astype(jnp.bfloat16).astype(jnp.float32)
         rest = stat - high
@@ -195,28 +197,32 @@
         low = rest - middle
         third = jnp.where(piece < 3, piece, piece - 3)
         cuts = jnp.where(third == 0, high, jnp.where(third == 1, middle, low))
-        sent[slots, :, width:] = cuts.astype(jnp.bfloat16).reshape(plane, rows, LANES)
-
+        sent[slots, :, width:] = cuts.astype(jnp.bfloat16).reshape(PLANES, rows, LANES)
+
+    for dz in range(1, PLANES):
+        query_copy(dz, 0).wait_recv()
+        for dp in range(1, plane):
+            query_copy(dz, dp, relayed=True).start()
     for copy in locals_:
         copy.wait()
 
-    for dz in range(PLANES):
-        for dp in peers(dz):
-            query_copy(dz, dp).wait_recv()
-        weigh(dz)
-        for dp in peers(dz):
+    for dp in range(plane):
+        if dp:
+            for dz in range(PLANES):
+                query_copy(dz, dp).wait_recv()
+        weigh(dp)
+        for dz in range(0 if dp else 1, PLANES):
             part_copy(dz, dp).start()
     received[0] = sent[0]
 
     for kind in range(2):
         for dz in range(1, PLANES):
             col_copy(kind, dz).wait_recv()
-        for dp in peers(0):
+        for dp in range(1, plane):
             plane_copy(kind, dp).start()
 
-    for dz in range(PLANES):
-        for dp in peers(dz):
-            part_copy(dz, dp).wait_recv()
+    for dz, dp in others:
+        part_copy(dz, dp).wait_recv()
 
     stats = received[:, :, width:].astype(jnp.float32).reshape(owners * rows, LANES)
     stats = (
@@ -254,16 +260,15 @@
 
     for step in range(1, head_devices):
         square_copy(step).start()
-    for dz in range(PLANES):
-        for dp in peers(dz):
-            query_copy(dz, dp).wait_send()
-            part_copy(dz, dp).wait_send()
+    for dz, dp in others:
+        query_copy(dz, dp).wait_send()
+        part_copy(dz, dp).wait_send()
     moment = lax.broadcasted_iota(jnp.int32, gate.shape, 0) == step_ref[0]
     gate_row = jnp.sum(jnp.where(moment, gate[...], 0.0), axis=0, keepdims=True)
     for kind in range(2):
         for dz in range(1, PLANES):
             col_copy(kind, dz).wait_send()
-        for dp in peers(0):
+        for dp in range(1, plane):
             plane_copy(kind, dp).wait_recv()
     for dz in range(PLANES):
         z = lax.rem(my_z - dz + PLANES, PLANES)
@@ -271,6 +276,12 @@
             p = lax.rem(my_p - dp + plane, plane)
             all_keys[z, p] = gath_key[dp, dz]
             all_values[z, p] = gath_value[dp, dz]
+    handed = [
+        pltpu.make_async_copy(all_keys, keys_out, local_sem.at[0]),
+        pltpu.make_async_copy(all_values, values_out, local_sem.at[1]),
+    ]
+    for copy in handed:
+        copy.start()
     for step in range(1, head_devices):
         square_copy(step).wait_recv()
     mean = jnp.sum(squares[...], axis=0) * (1.0 / (width * head_devices))
@@ -282,8 +293,41 @@
     for step in range(1, head_devices):
         square_copy(step).wait_send()
     for kind in range(2):
-        for dp in peers(0):
+        for dp in range(1, plane):
             plane_copy(kind, dp).wait_send()
+    for copy in handed:
+        copy.wait()
+
+
+def finish(
+    evictor_ref,
+    attended_in,
+    all_keys,
+    all_values,
+    cache_key_in,
+    cache_value_in,
+    out_ref,
+    next_key,
+    next_value,
+    sem,
+):
+    output = pltpu.make_async_copy(attended_in, out_ref, sem.at[0])
+    output.start()
+
+    def roll(key_from, value_from):
+        moves = [
+            pltpu.make_async_copy(key_from, next_key, sem.at[1]),
+            pltpu.make_async_copy(value_from, next_value, sem.at[2]),
+        ]
+        for move in moves:
+            move.start()
+        for move in moves:
+            move.wait()
+
+    evicted = lax.axis_index("ctx") == evictor_ref[0]
+    pl.when(evicted)(lambda: roll(all_keys, all_values))
+    pl.when(jnp.logical_not(evicted))(lambda: roll(cache_key_in, cache_value_in))
+    output.wait()
 
 
 def body(
@@ -314,8 +358,10 @@
         functools.partial(kernel, owners, head_devices),
         out_shape=(jax.ShapeDtypeStruct((rows, width), bf16), gathered, gathered),
         in_specs=[smem] * 3 + [anywhere] * 6,
-        out_specs=(vmem, vmem, vmem),
+        out_specs=(vmem, anywhere, anywhere),
         scratch_shapes=[
+            pltpu.VMEM(gathered.shape, bf16),
+            pltpu.VMEM(gathered.shape, bf16),
             pltpu.VMEM((plane, PLANES, rows, width), bf16),
             pltpu.VMEM((plane, PLANES, rows, width), bf16),
             pltpu.VMEM((owners, rows, width), bf16),
@@ -352,13 +398,23 @@
         cache_value,
         time_gate,
     )
-    evicted = lax.axis_index("ctx") == evictor[0]
-
-    def rolled(gathered, cache):
-        return jnp.where(evicted, gathered.reshape(cache.shape), cache)
-
-    next_key, next_value = rolled(fresh_keys, cache_key), rolled(fresh_values, cache_value)
-    return (attn_output, next_key, next_value)
+    cache_shape = jax.ShapeDtypeStruct(cache_key.shape, bf16)
+    return pl.pallas_call(
+        finish,
+        out_shape=(jax.ShapeDtypeStruct((rows, width), bf16), cache_shape, cache_shape),
+        in_specs=[smem] + [anywhere] * 5,
+        out_specs=(anywhere, anywhere, anywhere),
+        scratch_shapes=[dma((3,))],
+        compiler_params=pltpu.CompilerParams(vmem_limit_bytes=60 * 1024 * 1024),
+        name="finish",
+    )(
+        evictor,
+        attn_output,
+        fresh_keys.reshape(cache_key.shape),
+        fresh_values.reshape(cache_value.shape),
+        cache_key,
+        cache_value,
+    )
 
 
 def solution(mesh):

time: 33.8 us -> 40.7 us (1.20)
  Pallas kernels: 29.2 us -> 38.6 us
  other arithmetic: 1.82 us -> 0 us
  local copies, waits for them, and re-layouts: 0.61 us -> 0 us
    pallas_call x0 -> x1, Pallas kernels: none -> 13.4 us  [body(): pl.pallas_call(finish, out_shape=(jax.ShapeDtypeStruct((rows, width), bf1...]
    pallas_call x1, Pallas kernels: 29.2 us -> 25.2 us  [body(): pl.pallas_call(functools.partial(kernel, owners, head_devices), out_shape...]
    select_n x1 -> x0, other arithmetic: 1.82 us -> none  [rolled(): return jnp.where(evicted, gathered.reshape(cache.shape), cache)]
    unnamed x7 -> x0, local copies, waits for them, and re-layouts: 0.61 us -> none
where the time goes in v2:
time: 40.7 us; the launch traced here: 40.6 us
  Pallas kernels  38.6 us (95%)
  between operations  1.93 us (5%)
    pallas_call x1, Pallas kernels, body(): pl.pallas_call(functools.partial(kernel, owners, head_devices), out_shape...  25.2 us
    pallas_call x1, Pallas kernels, body(): pl.pallas_call(finish, out_shape=(jax.ShapeDtypeStruct((rows, width), bf1...  13.4 us

profile of v2, /device:TPU:0, one launch (start us, length us, event | category | flops | bytes accessed | tf_op | source)
XLA Modules:
  0.0 40.6 jit_solution(13606442688418994582)
XLA Ops:
  1.9 25.2 %attend.1 = (bf16[16,384]{1,0:T(8,128)(2,1)}, bf16[4,4,16,384]{3,2,1,0:T(8,128)(2,1)}, bf16[4,4,16,384]{3,2,1,0:T(8,128)(2,1)}) custom-call(s32[16]{0:T(128)} %slot_ref.1, s32[1]{0:T(128)S(6)} %copy.14.step_ref, f32[3]{0:T(128)} %slope_ref.1, bf16[16,384]{1,0:T(8,128)(2,1)} %query_in.1, bf16[16,384]{1,0:T(8,128)(2,1)} %key_in.1, bf16[16,384]{1,0:T(8,128)(2,1)} %value_in.1, ...), custom_call_target="tpu_custom_call" | custom-call | tf_op jit(solution)/shard_map/attend/pallas_call | solution.py:357
  27.1 13.4 %finish.1 = (bf16[16,384]{1,0:T(8,128)(2,1)}, bf16[256,384]{1,0:T(8,128)(2,1)}, bf16[256,384]{1,0:T(8,128)(2,1)}) custom-call(s32[1]{0:T(128)S(6)} %copy.13.evictor_ref, bf16[16,384]{1,0:T(8,128)(2,1)} %get-tuple-element.6.attended_in, bf16[256,384]{1,0:T(8,128)(2,1)} %bitcast.2, bf16[256,384]{1,0:T(8,128)(2,1)} %bitcast.3, bf16[256,384]{1,0:T(8,128)(2,1)} %cache_key_in.3, ...), custom_call_target="tpu_custom_call" | custom-call | tf_op jit(solution)/shard_map/finish/pallas_call | solution.py:402

commit v3 on v2

--- a/solution.py
+++ b/solution.py
@@ -16,9 +16,9 @@
 def kernel(
     owners,
     head_devices,
-    slot_ref,
-    step_ref,
-    slope_ref,
+    slot_in,
+    step_in,
+    slope_in,
     query_in,
     key_in,
     value_in,
@@ -39,6 +39,11 @@
     sent,
     received,
     squares,
+    slot_ref,
+    step_ref,
+    slope_ref,
+    flat_keys,
+    wide_values,
     local_sem,
     query_send,
     query_recv,
@@ -83,6 +88,9 @@
         pltpu.make_async_copy(gate_in, gate, local_sem.at[5]),
         pltpu.make_async_copy(key_in, gath_key.at[0, 0], local_sem.at[6]),
         pltpu.make_async_copy(value_in, gath_value.at[0, 0], local_sem.at[7]),
+        pltpu.make_async_copy(slot_in, slot_ref, local_sem.at[8]),
+        pltpu.make_async_copy(step_in, step_ref, local_sem.at[9]),
+        pltpu.make_async_copy(slope_in, slope_ref, local_sem.at[10]),
     ]
     for copy in locals_:
         copy.start()
@@ -149,6 +157,8 @@
         for kind in range(2):
             col_copy(kind, dz).start()
 
+    for copy in locals_:
+        copy.wait()
     slot_rank = jnp.int32(0)
     for slot in range(owners):
         slot_rank += jnp.where(slot_ref[slot] == me, slot, 0)
@@ -158,7 +168,11 @@
     column = lax.broadcasted_iota(jnp.int32, (1, key_rows), 1)
     lane = lax.broadcasted_iota(jnp.int32, (tokens, LANES), 1)
     group, piece = lane >> 3, lane & 7
-    ones = jnp.ones((key_rows, LANES), jnp.bfloat16)
+    for head in range(heads):
+        cut = slice(head * head_dim, (head + 1) * head_dim)
+        flat_keys[cut, :] = keys[:, cut].T
+        wide_values[head, :, :head_dim] = values[:, cut]
+        wide_values[head, :, head_dim:] = jnp.ones((key_rows, LANES), jnp.bfloat16)
 
     def weigh(dp):
         slots = slice(dp * PLANES, (dp + 1) * PLANES)
@@ -172,22 +186,13 @@
                 jnp.where(column < cache_rows + rows, 0.0, 1e30),
             )
             scores = (
-                lax.dot_general(
-                    query[:, cut],
-                    keys[:, cut],
-                    (((1,), (1,)), ((), ())),
-                    preferred_element_type=jnp.float32,
-                )
+                jnp.dot(query[:, cut], flat_keys[cut, :], preferred_element_type=jnp.float32)
                 * scale
                 - penalty
             )
             largest = jnp.max(scores, axis=1, keepdims=True)
             weights = jnp.exp(scores - largest).astype(jnp.bfloat16)
-            both = jnp.dot(
-                weights,
-                jnp.concatenate([values[:, cut], ones], axis=1),
-                preferred_element_type=jnp.float32,
-            )
+            both = jnp.dot(weights, wide_values[head], preferred_element_type=jnp.float32)
             numer, denom = both[:, :head_dim], both[:, head_dim:]
             sent[slots, :, cut] = numer.astype(jnp.bfloat16).reshape(PLANES, rows, head_dim)
             stat = jnp.where(group == head, jnp.where(piece < 3, largest, denom), stat)
@@ -203,8 +208,6 @@
         query_copy(dz, 0).wait_recv()
         for dp in range(1, plane):
             query_copy(dz, dp, relayed=True).start()
-    for copy in locals_:
-        copy.wait()
 
     for dp in range(plane):
         if dp:
@@ -309,25 +312,37 @@
     out_ref,
     next_key,
     next_value,
+    attended,
+    held,
     sem,
 ):
-    output = pltpu.make_async_copy(attended_in, out_ref, sem.at[0])
-    output.start()
+    first = pltpu.make_async_copy(attended_in, attended, sem.at[0])
+    first.start()
 
     def roll(key_from, value_from):
-        moves = [
-            pltpu.make_async_copy(key_from, next_key, sem.at[1]),
-            pltpu.make_async_copy(value_from, next_value, sem.at[2]),
+        loads = [
+            pltpu.make_async_copy(key_from, held.at[0], sem.at[1]),
+            pltpu.make_async_copy(value_from, held.at[1], sem.at[2]),
         ]
-        for move in moves:
-            move.start()
-        for move in moves:
-            move.wait()
+        stores = [
+            pltpu.make_async_copy(held.at[0], next_key, sem.at[1]),
+            pltpu.make_async_copy(held.at[1], next_value, sem.at[2]),
+        ]
+        output = pltpu.make_async_copy(attended, out_ref, sem.at[0])
+        for load in loads:
+            load.start()
+        first.wait()
+        output.start()
+        for load, store in zip(loads, stores):
+            load.wait()
+            store.start()
+        output.wait()
+        for store in stores:
+            store.wait()
 
     evicted = lax.axis_index("ctx") == evictor_ref[0]
     pl.when(evicted)(lambda: roll(all_keys, all_values))
     pl.when(jnp.logical_not(evicted))(lambda: roll(cache_key_in, cache_value_in))
-    output.wait()
 
 
 def body(
@@ -347,6 +362,7 @@
     owners = lax.axis_size("ctx")
     head_devices = lax.axis_size("head")
     plane = owners // PLANES
+    heads = age_slope.shape[0]
     key_rows = cache_rows + LANES * pl.cdiv(rows, LANES)
     smem = pl.BlockSpec(memory_space=pltpu.SMEM)
     vmem = pl.BlockSpec(memory_space=pltpu.VMEM)
@@ -357,7 +373,7 @@
     attn_output, fresh_keys, fresh_values = pl.pallas_call(
         functools.partial(kernel, owners, head_devices),
         out_shape=(jax.ShapeDtypeStruct((rows, width), bf16), gathered, gathered),
-        in_specs=[smem] * 3 + [anywhere] * 6,
+        in_specs=[anywhere] * 9,
         out_specs=(vmem, anywhere, anywhere),
         scratch_shapes=[
             pltpu.VMEM(gathered.shape, bf16),
@@ -371,7 +387,12 @@
             pltpu.VMEM((owners, rows, width + LANES), bf16),
             pltpu.VMEM((owners, rows, width + LANES), bf16),
             pltpu.VMEM((head_devices, rows, LANES), jnp.float32),
-            dma((8,)),
+            pltpu.SMEM(slot_owner.shape, jnp.int32),
+            pltpu.SMEM(timestep.shape, jnp.int32),
+            pltpu.SMEM(age_slope.shape, jnp.float32),
+            pltpu.VMEM((width, key_rows), bf16),
+            pltpu.VMEM((heads, key_rows, width // heads + LANES), bf16),
+            dma((11,)),
             dma((owners,)),
             dma((owners,)),
             dma((owners,)),
@@ -404,7 +425,11 @@
         out_shape=(jax.ShapeDtypeStruct((rows, width), bf16), cache_shape, cache_shape),
         in_specs=[smem] + [anywhere] * 5,
         out_specs=(anywhere, anywhere, anywhere),
-        scratch_shapes=[dma((3,))],
+        scratch_shapes=[
+            pltpu.VMEM((rows, width), bf16),
+            pltpu.VMEM((2,) + cache_key.shape, bf16),
+            dma((3,)),
+        ],
         compiler_params=pltpu.CompilerParams(vmem_limit_bytes=60 * 1024 * 1024),
         name="finish",
     )(

time: 40.7 us -> 27.7 us (0.68)
  Pallas kernels: 38.6 us -> 25.6 us
    pallas_call x1, Pallas kernels: 13.4 us -> 1.74 us  [body(): pl.pallas_call(finish, out_shape=(jax.ShapeDtypeStruct((rows, width), bf1...]
    pallas_call x1, Pallas kernels: 25.2 us -> 23.8 us  [body(): pl.pallas_call(functools.partial(kernel, owners, head_devices), out_shape...]
where the time goes in v3:
time: 27.7 us; the launch traced here: 27.5 us
  Pallas kernels  25.6 us (92%)
  between operations  1.93 us (7%)
    pallas_call x1, Pallas kernels, body(): pl.pallas_call(functools.partial(kernel, owners, head_devices), out_shape...  23.8 us
    pallas_call x1, Pallas kernels, body(): pl.pallas_call(finish, out_shape=(jax.ShapeDtypeStruct((rows, width), bf1...  1.74 us

profile of v3, /device:TPU:0, one launch (start us, length us, event | category | flops | bytes accessed | tf_op | source)
XLA Modules:
  0.0 27.5 jit_solution(1139723127369177329)
XLA Ops:
  1.9 23.8 %attend.1 = (bf16[16,384]{1,0:T(8,128)(2,1)}, bf16[4,4,16,384]{3,2,1,0:T(8,128)(2,1)}, bf16[4,4,16,384]{3,2,1,0:T(8,128)(2,1)}) custom-call(s32[16]{0:T(128)} %slot_in.1, s32[1]{0:T(128)S(6)} %copy.14.step_in, f32[3]{0:T(128)} %slope_in.1, bf16[16,384]{1,0:T(8,128)(2,1)} %query_in.1, bf16[16,384]{1,0:T(8,128)(2,1)} %key_in.1, bf16[16,384]{1,0:T(8,128)(2,1)} %value_in.1, ...), custom_call_target="tpu_custom_call" | custom-call | tf_op jit(solution)/shard_map/attend/pallas_call | solution.py:373
  25.7 1.7 %finish.1 = (bf16[16,384]{1,0:T(8,128)(2,1)}, bf16[256,384]{1,0:T(8,128)(2,1)}, bf16[256,384]{1,0:T(8,128)(2,1)}) custom-call(s32[1]{0:T(128)S(6)} %copy.13.evictor_ref, bf16[16,384]{1,0:T(8,128)(2,1)} %get-tuple-element.6.attended_in, bf16[256,384]{1,0:T(8,128)(2,1)} %bitcast.2, bf16[256,384]{1,0:T(8,128)(2,1)} %bitcast.3, bf16[256,384]{1,0:T(8,128)(2,1)} %cache_key_in.3, ...), custom_call_target="tpu_custom_call" | custom-call | tf_op jit(solution)/shard_map/finish/pallas_call | solution.py:423

commit v4 on v3

--- a/solution.py
+++ b/solution.py
@@ -30,8 +30,7 @@
     values_out,
     all_keys,
     all_values,
-    gath_key,
-    gath_value,
+    gathered,
     queries,
     keys,
     values,
@@ -86,8 +85,8 @@
         pltpu.make_async_copy(cache_value_in, values.at[pl.ds(0, cache_rows)], local_sem.at[3]),
         pltpu.make_async_copy(value_in, values.at[pl.ds(cache_rows, rows)], local_sem.at[4]),
         pltpu.make_async_copy(gate_in, gate, local_sem.at[5]),
-        pltpu.make_async_copy(key_in, gath_key.at[0, 0], local_sem.at[6]),
-        pltpu.make_async_copy(value_in, gath_value.at[0, 0], local_sem.at[7]),
+        pltpu.make_async_copy(key_in, gathered.at[0, 0, 0], local_sem.at[6]),
+        pltpu.make_async_copy(value_in, gathered.at[0, 0, 1], local_sem.at[7]),
         pltpu.make_async_copy(slot_in, slot_ref, local_sem.at[8]),
         pltpu.make_async_copy(step_in, step_ref, local_sem.at[9]),
         pltpu.make_async_copy(slope_in, slope_ref, local_sem.at[10]),
@@ -100,52 +99,52 @@
 
     pl.semaphore_wait(barrier, owners - 1 + head_devices - 1)
 
+    def wrapped(index, size):
+        if size & (size - 1):
+            return lax.rem(index + size, size)
+        return index & (size - 1)
+
     def device(dz, dp):
-        z = lax.rem(my_z + dz + PLANES, PLANES)
-        return (z * plane + lax.rem(my_p + dp + plane, plane), my_head)
-
-    def query_copy(dz, dp, relayed=False):
-        slot = dp * PLANES + dz
+        z = wrapped(my_z + dz, PLANES)
+        return (z * plane + wrapped(my_p + dp, plane), my_head)
+
+    def send(source, target, sems, index, where):
         return pltpu.make_async_remote_copy(
-            src_ref=queries.at[dz] if relayed else query_in,
-            dst_ref=queries.at[slot],
-            send_sem=query_send.at[slot],
-            recv_sem=query_recv.at[slot],
-            device_id=device(0 if relayed else dz, dp),
+            src_ref=source,
+            dst_ref=target,
+            send_sem=sems[0].at[index],
+            recv_sem=sems[1].at[index],
+            device_id=where,
             device_id_type=MESH,
         )
 
+    def query_copy(dz, dp):
+        slot = dp * PLANES + dz
+        sems = (query_send, query_recv)
+        return send(query_in, queries.at[slot], sems, slot, device(dz, dp))
+
+    def relay_copy(dp):
+        slot = dp * PLANES + 1
+        return send(
+            queries.at[pl.ds(1, PLANES - 1)],
+            queries.at[pl.ds(slot, PLANES - 1)],
+            (query_send, query_recv),
+            slot,
+            device(0, dp),
+        )
+
     def part_copy(dz, dp):
         slot = dp * PLANES + dz
-        return pltpu.make_async_remote_copy(
-            src_ref=sent.at[slot],
-            dst_ref=received.at[slot],
-            send_sem=part_send.at[slot],
-            recv_sem=part_recv.at[slot],
-            device_id=device(-dz, -dp),
-            device_id_type=MESH,
-        )
-
-    def col_copy(kind, dz):
-        return pltpu.make_async_remote_copy(
-            src_ref=(key_in, value_in)[kind],
-            dst_ref=(gath_key, gath_value)[kind].at[0, dz],
-            send_sem=col_send.at[kind * PLANES + dz],
-            recv_sem=col_recv.at[kind * PLANES + dz],
-            device_id=device(dz, 0),
-            device_id_type=MESH,
-        )
-
-    def plane_copy(kind, dp):
-        gathered = (gath_key, gath_value)[kind]
-        return pltpu.make_async_remote_copy(
-            src_ref=gathered.at[0],
-            dst_ref=gathered.at[dp],
-            send_sem=plane_send.at[kind * plane + dp],
-            recv_sem=plane_recv.at[kind * plane + dp],
-            device_id=device(0, dp),
-            device_id_type=MESH,
-        )
+        sems = (part_send, part_recv)
+        return send(sent.at[slot], received.at[slot], sems, slot, device(-dz, -dp))
+
+    def col_copy(dz):
+        sems = (col_send, col_recv)
+        return send(gathered.at[0, 0], gathered.at[0, dz], sems, dz, device(dz, 0))
+
+    def plane_copy(dp):
+        sems = (plane_send, plane_recv)
+        return send(gathered.at[0], gathered.at[dp], sems, dp, device(0, dp))
 
     others = [(dz, dp) for dp in range(plane) for dz in range(PLANES) if dz or dp]
 
@@ -153,12 +152,11 @@
         query_copy(dz, 0).start()
     for dp in range(1, plane):
         query_copy(0, dp).start()
-    for dz in range(1, PLANES):
-        for kind in range(2):
-            col_copy(kind, dz).start()
-
     for copy in locals_:
         copy.wait()
+    for dz in range(1, PLANES):
+        col_copy(dz).start()
+
     slot_rank = jnp.int32(0)
     for slot in range(owners):
         slot_rank += jnp.where(slot_ref[slot] == me, slot, 0)
@@ -206,23 +204,22 @@
 
     for dz in range(1, PLANES):
         query_copy(dz, 0).wait_recv()
-        for dp in range(1, plane):
-            query_copy(dz, dp, relayed=True).start()
+    for dp in range(1, plane):
+        relay_copy(dp).start()
 
     for dp in range(plane):
         if dp:
-            for dz in range(PLANES):
-                query_copy(dz, dp).wait_recv()
+            query_copy(0, dp).wait_recv()
+            relay_copy(dp).wait_recv()
         weigh(dp)
         for dz in range(0 if dp else 1, PLANES):
             part_copy(dz, dp).start()
     received[0] = sent[0]
 
-    for kind in range(2):
-        for dz in range(1, PLANES):
-            col_copy(kind, dz).wait_recv()
-        for dp in range(1, plane):
-            plane_copy(kind, dp).start()
+    for dz in range(1, PLANES):
+        col_copy(dz).wait_recv()
+    for dp in range(1, plane):
+        plane_copy(dp).start()
 
     for dz, dp in others:
         part_copy(dz, dp).wait_recv()
@@ -252,33 +249,29 @@
     squares[0] = jnp.broadcast_to(jnp.sum(total, axis=1, keepdims=True), (rows, LANES))
 
     def square_copy(step):
-        return pltpu.make_async_remote_copy(
-            src_ref=squares.at[0],
-            dst_ref=squares.at[step],
-            send_sem=square_send.at[step],
-            recv_sem=square_recv.at[step],
-            device_id=(me, lax.rem(my_head + step, head_devices)),
-            device_id_type=MESH,
-        )
+        where = (me, wrapped(my_head + step, head_devices))
+        return send(squares.at[0], squares.at[step], (square_send, square_recv), step, where)
 
     for step in range(1, head_devices):
         square_copy(step).start()
+    for dz in range(1, PLANES):
+        query_copy(dz, 0).wait_send()
+        col_copy(dz).wait_send()
+    for dp in range(1, plane):
+        query_copy(0, dp).wait_send()
+        relay_copy(dp).wait_send()
     for dz, dp in others:
-        query_copy(dz, dp).wait_send()
         part_copy(dz, dp).wait_send()
     moment = lax.broadcasted_iota(jnp.int32, gate.shape, 0) == step_ref[0]
     gate_row = jnp.sum(jnp.where(moment, gate[...], 0.0), axis=0, keepdims=True)
-    for kind in range(2):
-        for dz in range(1, PLANES):
-            col_copy(kind, dz).wait_send()
-        for dp in range(1, plane):
-            plane_copy(kind, dp).wait_recv()
+    for dp in range(1, plane):
+        plane_copy(dp).wait_recv()
     for dz in range(PLANES):
-        z = lax.rem(my_z - dz + PLANES, PLANES)
+        z = wrapped(my_z - dz, PLANES)
         for dp in range(plane):
-            p = lax.rem(my_p - dp + plane, plane)
-            all_keys[z, p] = gath_key[dp, dz]
-            all_values[z, p] = gath_value[dp, dz]
+            p = wrapped(my_p - dp, plane)
+            all_keys[z, p] = gathered[dp, dz, 0]
+            all_values[z, p] = gathered[dp, dz, 1]
     handed = [
         pltpu.make_async_copy(all_keys, keys_out, local_sem.at[0]),
         pltpu.make_async_copy(all_values, values_out, local_sem.at[1]),
@@ -295,9 +288,8 @@
 
     for step in range(1, head_devices):
         square_copy(step).wait_send()
-    for kind in range(2):
-        for dp in range(1, plane):
-            plane_copy(kind, dp).wait_send()
+    for dp in range(1, plane):
+        plane_copy(dp).wait_send()
     for copy in handed:
         copy.wait()
 
@@ -378,8 +370,7 @@
         scratch_shapes=[
             pltpu.VMEM(gathered.shape, bf16),
             pltpu.VMEM(gathered.shape, bf16),
-            pltpu.VMEM((plane, PLANES, rows, width), bf16),
-            pltpu.VMEM((plane, PLANES, rows, width), bf16),
+            pltpu.VMEM((plane, PLANES, 2, rows, width), bf16),
             pltpu.VMEM((owners, rows, width), bf16),
             pltpu.VMEM((key_rows, width), bf16),
             pltpu.VMEM((key_rows, width), bf16),
@@ -397,10 +388,10 @@
             dma((owners,)),
             dma((owners,)),
             dma((owners,)),
-            dma((2 * PLANES,)),
-            dma((2 * PLANES,)),
-            dma((2 * plane,)),
-            dma((2 * plane,)),
+            dma((PLANES,)),
+            dma((PLANES,)),
+            dma((plane,)),
+            dma((plane,)),
             dma((head_devices,)),
             dma((head_devices,)),
         ],

time: 27.7 us -> 28.1 us (1.014)
  Pallas kernels: 25.6 us -> 26 us
    pallas_call x1, Pallas kernels: 23.8 us -> 24.2 us  [body(): pl.pallas_call(functools.partial(kernel, owners, head_devices), out_shape...]
where the time goes in v4:
time: 28.1 us; the launch traced here: 27.9 us
  Pallas kernels  26 us (93%)
  between operations  1.93 us (7%)
    pallas_call x1, Pallas kernels, body(): pl.pallas_call(functools.partial(kernel, owners, head_devices), out_shape...  24.2 us
    pallas_call x1, Pallas kernels, body(): pl.pallas_call(finish, out_shape=(jax.ShapeDtypeStruct((rows, width), bf1...  1.74 us

profile of v4, /device:TPU:0, one launch (start us, length us, event | category | flops | bytes accessed | tf_op | source)
XLA Modules:
  0.0 27.9 jit_solution(13927623124868632363)
XLA Ops:
  1.9 24.2 %attend.1 = (bf16[16,384]{1,0:T(8,128)(2,1)}, bf16[4,4,16,384]{3,2,1,0:T(8,128)(2,1)}, bf16[4,4,16,384]{3,2,1,0:T(8,128)(2,1)}) custom-call(s32[16]{0:T(128)} %slot_in.1, s32[1]{0:T(128)S(6)} %copy.14.step_in, f32[3]{0:T(128)} %slope_in.1, bf16[16,384]{1,0:T(8,128)(2,1)} %query_in.1, bf16[16,384]{1,0:T(8,128)(2,1)} %key_in.1, bf16[16,384]{1,0:T(8,128)(2,1)} %value_in.1, ...), custom_call_target="tpu_custom_call" | custom-call | tf_op jit(solution)/shard_map/attend/pallas_call | solution.py:365
  26.1 1.7 %finish.1 = (bf16[16,384]{1,0:T(8,128)(2,1)}, bf16[256,384]{1,0:T(8,128)(2,1)}, bf16[256,384]{1,0:T(8,128)(2,1)}) custom-call(s32[1]{0:T(128)S(6)} %copy.13.evictor_ref, bf16[16,384]{1,0:T(8,128)(2,1)} %get-tuple-element.6.attended_in, bf16[256,384]{1,0:T(8,128)(2,1)} %bitcast.2, bf16[256,384]{1,0:T(8,128)(2,1)} %bitcast.3, bf16[256,384]{1,0:T(8,128)(2,1)} %cache_key_in.3, ...), custom_call_target="tpu_custom_call" | custom-call | tf_op jit(solution)/shard_map/finish/pallas_call | solution.py:414

commit v5 on v4

--- a/solution.py
+++ b/solution.py
@@ -214,12 +214,12 @@
         weigh(dp)
         for dz in range(0 if dp else 1, PLANES):
             part_copy(dz, dp).start()
+        if dp == 0:
+            for dz in range(1, PLANES):
+                col_copy(dz).wait_recv()
+            for peer in range(1, plane):
+                plane_copy(peer).start()
     received[0] = sent[0]
-
-    for dz in range(1, PLANES):
-        col_copy(dz).wait_recv()
-    for dp in range(1, plane):
-        plane_copy(dp).start()
 
     for dz, dp in others:
         part_copy(dz, dp).wait_recv()

time: 28.1 us -> 28.9 us (1.028)
  Pallas kernels: 26 us -> 26.7 us
    pallas_call x1, Pallas kernels: 24.2 us -> 24.9 us  [body(): pl.pallas_call(functools.partial(kernel, owners, head_devices), out_shape...]
where the time goes in v5:
time: 28.9 us; the launch traced here: 28.6 us
  Pallas kernels  26.7 us (92%)
  between operations  1.93 us (7%)
    pallas_call x1, Pallas kernels, body(): pl.pallas_call(functools.partial(kernel, owners, head_devices), out_shape...  24.9 us
    pallas_call x1, Pallas kernels, body(): pl.pallas_call(finish, out_shape=(jax.ShapeDtypeStruct((rows, width), bf1...  1.74 us

profile of v5, /device:TPU:0, one launch (start us, length us, event | category | flops | bytes accessed | tf_op | source)
XLA Modules:
  0.0 28.6 jit_solution(16120900064858402695)
XLA Ops:
  1.9 24.9 %attend.1 = (bf16[16,384]{1,0:T(8,128)(2,1)}, bf16[4,4,16,384]{3,2,1,0:T(8,128)(2,1)}, bf16[4,4,16,384]{3,2,1,0:T(8,128)(2,1)}) custom-call(s32[16]{0:T(128)} %slot_in.1, s32[1]{0:T(128)S(6)} %copy.14.step_in, f32[3]{0:T(128)} %slope_in.1, bf16[16,384]{1,0:T(8,128)(2,1)} %query_in.1, bf16[16,384]{1,0:T(8,128)(2,1)} %key_in.1, bf16[16,384]{1,0:T(8,128)(2,1)} %value_in.1, ...), custom_call_target="tpu_custom_call" | custom-call | tf_op jit(solution)/shard_map/attend/pallas_call | solution.py:365
  26.9 1.7 %finish.1 = (bf16[16,384]{1,0:T(8,128)(2,1)}, bf16[256,384]{1,0:T(8,128)(2,1)}, bf16[256,384]{1,0:T(8,128)(2,1)}) custom-call(s32[1]{0:T(128)S(6)} %copy.13.evictor_ref, bf16[16,384]{1,0:T(8,128)(2,1)} %get-tuple-element.6.attended_in, bf16[256,384]{1,0:T(8,128)(2,1)} %bitcast.2, bf16[256,384]{1,0:T(8,128)(2,1)} %bitcast.3, bf16[256,384]{1,0:T(8,128)(2,1)} %cache_key_in.3, ...), custom_call_target="tpu_custom_call" | custom-call | tf_op jit(solution)/shard_map/finish/pallas_call | solution.py:414

commit v6 on v4

--- a/solution.py
+++ b/solution.py
@@ -162,9 +162,8 @@
         slot_rank += jnp.where(slot_ref[slot] == me, slot, 0)
     age = (slot_rank + 1).astype(jnp.float32) * (1.0 / owners)
     scale = 1.0 / math.sqrt(head_dim)
-    tokens = PLANES * rows
     column = lax.broadcasted_iota(jnp.int32, (1, key_rows), 1)
-    lane = lax.broadcasted_iota(jnp.int32, (tokens, LANES), 1)
+    lane = lax.broadcasted_iota(jnp.int32, (1, LANES), 1)
     group, piece = lane >> 3, lane & 7
     for head in range(heads):
         cut = slice(head * head_dim, (head + 1) * head_dim)
@@ -172,8 +171,10 @@
         wide_values[head, :, :head_dim] = values[:, cut]
         wide_values[head, :, head_dim:] = jnp.ones((key_rows, LANES), jnp.bfloat16)
 
-    def weigh(dp):
-        slots = slice(dp * PLANES, (dp + 1) * PLANES)
+    def weigh(columns):
+        count = len(columns) * PLANES
+        tokens = count * rows
+        slots = slice(columns[0] * PLANES, columns[0] * PLANES + count)
         query = queries[slots].reshape(tokens, width)
         stat = jnp.zeros((tokens, LANES), jnp.float32)
         for head in range(heads):
@@ -192,7 +193,7 @@
             weights = jnp.exp(scores - largest).astype(jnp.bfloat16)
             both = jnp.dot(weights, wide_values[head], preferred_element_type=jnp.float32)
             numer, denom = both[:, :head_dim], both[:, head_dim:]
-            sent[slots, :, cut] = numer.astype(jnp.bfloat16).reshape(PLANES, rows, head_dim)
+            sent[slots, :, cut] = numer.astype(jnp.bfloat16).reshape(count, rows, head_dim)
             stat = jnp.where(group == head, jnp.where(piece < 3, largest, denom), stat)
         high = stat.astype(jnp.bfloat16).astype(jnp.float32)
         rest = stat - high
@@ -200,20 +201,23 @@
         low = rest - middle
         third = jnp.where(piece < 3, piece, piece - 3)
         cuts = jnp.where(third == 0, high, jnp.where(third == 1, middle, low))
-        sent[slots, :, width:] = cuts.astype(jnp.bfloat16).reshape(PLANES, rows, LANES)
+        sent[slots, :, width:] = cuts.astype(jnp.bfloat16).reshape(count, rows, LANES)
 
     for dz in range(1, PLANES):
         query_copy(dz, 0).wait_recv()
     for dp in range(1, plane):
         relay_copy(dp).start()
 
-    for dp in range(plane):
-        if dp:
-            query_copy(0, dp).wait_recv()
-            relay_copy(dp).wait_recv()
-        weigh(dp)
-        for dz in range(0 if dp else 1, PLANES):
-            part_copy(dz, dp).start()
+    batches = [range(1)] + [range(dp, min(dp + 3, plane)) for dp in range(1, plane, 3)]
+    for columns in batches:
+        for dp in columns:
+            if dp:
+                query_copy(0, dp).wait_recv()
+                relay_copy(dp).wait_recv()
+        weigh(columns)
+        for dp in columns:
+            for dz in range(0 if dp else 1, PLANES):
+                part_copy(dz, dp).start()
     received[0] = sent[0]
 
     for dz in range(1, PLANES):

time: 28.1 us -> 28.7 us (1.021)
  Pallas kernels: 26 us -> 26.6 us
    pallas_call x1, Pallas kernels: 24.2 us -> 24.8 us  [body(): pl.pallas_call(functools.partial(kernel, owners, head_devices), out_shape...]
where the time goes in v6:
time: 28.7 us; the launch traced here: 28.5 us
  Pallas kernels  26.6 us (93%)
  between operations  1.93 us (7%)
    pallas_call x1, Pallas kernels, body(): pl.pallas_call(functools.partial(kernel, owners, head_devices), out_shape...  24.8 us
    pallas_call x1, Pallas kernels, body(): pl.pallas_call(finish, out_shape=(jax.ShapeDtypeStruct((rows, width), bf1...  1.74 us

profile of v6, /device:TPU:0, one launch (start us, length us, event | category | flops | bytes accessed | tf_op | source)
XLA Modules:
  0.0 28.5 jit_solution(16817583257393619945)
XLA Ops:
  1.9 24.8 %attend.1 = (bf16[16,384]{1,0:T(8,128)(2,1)}, bf16[4,4,16,384]{3,2,1,0:T(8,128)(2,1)}, bf16[4,4,16,384]{3,2,1,0:T(8,128)(2,1)}) custom-call(s32[16]{0:T(128)} %slot_in.1, s32[1]{0:T(128)S(6)} %copy.14.step_in, f32[3]{0:T(128)} %slope_in.1, bf16[16,384]{1,0:T(8,128)(2,1)} %query_in.1, bf16[16,384]{1,0:T(8,128)(2,1)} %key_in.1, bf16[16,384]{1,0:T(8,128)(2,1)} %value_in.1, ...), custom_call_target="tpu_custom_call" | custom-call | tf_op jit(solution)/shard_map/attend/pallas_call | solution.py:369
  26.7 1.7 %finish.1 = (bf16[16,384]{1,0:T(8,128)(2,1)}, bf16[256,384]{1,0:T(8,128)(2,1)}, bf16[256,384]{1,0:T(8,128)(2,1)}) custom-call(s32[1]{0:T(128)S(6)} %copy.13.evictor_ref, bf16[16,384]{1,0:T(8,128)(2,1)} %get-tuple-element.6.attended_in, bf16[256,384]{1,0:T(8,128)(2,1)} %bitcast.2, bf16[256,384]{1,0:T(8,128)(2,1)} %bitcast.3, bf16[256,384]{1,0:T(8,128)(2,1)} %cache_key_in.3, ...), custom_call_target="tpu_custom_call" | custom-call | tf_op jit(solution)/shard_map/finish/pallas_call | solution.py:418

commit v7 on v3

--- a/solution.py
+++ b/solution.py
@@ -153,9 +153,6 @@
         query_copy(dz, 0).start()
     for dp in range(1, plane):
         query_copy(0, dp).start()
-    for dz in range(1, PLANES):
-        for kind in range(2):
-            col_copy(kind, dz).start()
 
     for copy in locals_:
         copy.wait()
@@ -208,6 +205,9 @@
         query_copy(dz, 0).wait_recv()
         for dp in range(1, plane):
             query_copy(dz, dp, relayed=True).start()
+    for dz in range(1, PLANES):
+        for kind in range(2):
+            col_copy(kind, dz).start()
 
     for dp in range(plane):
         if dp:

time: 27.7 us -> 27.9 us (level)
  no operation moved by 1% of the time
where the time goes in v7:
time: 27.9 us; the launch traced here: 27.6 us
  Pallas kernels  25.7 us (92%)
  between operations  1.93 us (7%)
    pallas_call x1, Pallas kernels, body(): pl.pallas_call(functools.partial(kernel, owners, head_devices), out_shape...  23.9 us
    pallas_call x1, Pallas kernels, body(): pl.pallas_call(finish, out_shape=(jax.ShapeDtypeStruct((rows, width), bf1...  1.74 us

profile of v7, /device:TPU:0, one launch (start us, length us, event | category | flops | bytes accessed | tf_op | source)
XLA Modules:
  0.0 27.6 jit_solution(7881559977158496258)
XLA Ops:
  1.9 23.9 %attend.1 = (bf16[16,384]{1,0:T(8,128)(2,1)}, bf16[4,4,16,384]{3,2,1,0:T(8,128)(2,1)}, bf16[4,4,16,384]{3,2,1,0:T(8,128)(2,1)}) custom-call(s32[16]{0:T(128)} %slot_in.1, s32[1]{0:T(128)S(6)} %copy.14.step_in, f32[3]{0:T(128)} %slope_in.1, bf16[16,384]{1,0:T(8,128)(2,1)} %query_in.1, bf16[16,384]{1,0:T(8,128)(2,1)} %key_in.1, bf16[16,384]{1,0:T(8,128)(2,1)} %value_in.1, ...), custom_call_target="tpu_custom_call" | custom-call | tf_op jit(solution)/shard_map/attend/pallas_call | solution.py:373
  25.9 1.7 %finish.1 = (bf16[16,384]{1,0:T(8,128)(2,1)}, bf16[256,384]{1,0:T(8,128)(2,1)}, bf16[256,384]{1,0:T(8,128)(2,1)}) custom-call(s32[1]{0:T(128)S(6)} %copy.13.evictor_ref, bf16[16,384]{1,0:T(8,128)(2,1)} %get-tuple-element.6.attended_in, bf16[256,384]{1,0:T(8,128)(2,1)} %bitcast.2, bf16[256,384]{1,0:T(8,128)(2,1)} %bitcast.3, bf16[256,384]{1,0:T(8,128)(2,1)} %cache_key_in.3, ...), custom_call_target="tpu_custom_call" | custom-call | tf_op jit(solution)/shard_map/finish/pallas_call | solution.py:423
